TPU v7x, 32 devices: a whole 2x2x4 slice. The times are simulated.
32 devices in a mesh: dp: 8 (over y, x, core), tensor: 4 (over z).
Axes of the slice: x: 2, y: 2, z: 4, core: 2. Of those that a mesh axis runs over, the one named last changes fastest.
Arguments:
- hidden_in: bfloat16 [6144, 2048], P('dp'), may hold values from -6 to 6
- segment_ids: int32 [6144], P('dp'), may hold values from 0 to 63, never falling along the last dimension, each value on 1 to 384 neighbouring positions
- modality: int32 [6144], P('dp'), may hold values from 0 to 1
- norm_gain: float32 [2048], replicated, may hold values from 0.5 to 1.5
- in_proj: bfloat16 [2, 2048, 2, 4096], P(None, None, None, 'tensor'), may hold values from -0.125 to 0.125
- conv_weight: float32 [4, 4096], P(None, 'tensor'), may hold values from -0.8 to 0.8
- conv_bias: float32 [4096], P('tensor'), may hold values from -1 to 1
- x_proj: bfloat16 [2, 4096, 160], P(None, 'tensor'), may hold values from -0.1875 to 0.1875
- dt_proj: bfloat16 [2, 128, 4096], P(None, None, 'tensor'), may hold values from -0.5 to 0.5
- dt_bias: float32 [2, 4096], P(None, 'tensor'), may hold values from -5 to -1
- a_log: float32 [16, 4096], P(None, 'tensor'), may hold values from -2 to 2.5
- skip_gain: float32 [4096], P('tensor'), may hold values from 0.5 to 1.5
- out_proj: bfloat16 [2, 4096, 2048], P(None, 'tensor'), may hold values from -0.1875 to 0.1875
- out_grad: bfloat16 [6144, 2048], P('dp'), may hold values from -6 to 6
Outputs:
- output: bfloat16 [6144, 2048], P('dp')
- input_grad: bfloat16 [6144, 2048], P('dp')
- norm_gain_grad: float32 [2048], replicated
- in_proj_grad: float32 [2, 2048, 2, 4096], P(None, None, None, 'tensor')
- conv_weight_grad: float32 [4, 4096], P(None, 'tensor')
- conv_bias_grad: float32 [4096], P('tensor')
- x_proj_grad: float32 [2, 4096, 160], P(None, 'tensor')
- dt_proj_grad: float32 [2, 128, 4096], P(None, None, 'tensor')
- dt_bias_grad: float32 [2, 4096], P(None, 'tensor')
- a_log_grad: float32 [16, 4096], P(None, 'tensor')
- skip_grad: float32 [4096], P('tensor')
- out_proj_grad: float32 [2, 4096, 2048], P(None, 'tensor')
Inputs may be any that keep to these rules, and one draw needn't show every extreme that they name: `segment_ids`: segment ids never fall along the tokens; a segment holds 1 to 384 tokens and one holds exactly that many.
All inputs are finite; a program needn't handle non-finite values.
Results may differ from a plain program's by a relative error of at most 0.011.
Values may be sent and summed in bfloat16 or wider, within the bound.
A program may use at most 320 MiB of HBM per device.

v0:
```python
import jax
import jax.numpy as jnp
from jax import lax
from jax.sharding import PartitionSpec as P

EPS = 1e-05


def lagged(values, offset):
    padding = [(offset, 0)] + [(0, 0)] * (values.ndim - 1)
    return jnp.pad(values, padding)[: values.shape[0]]


def leading(values, offset):
    padding = [(0, offset)] + [(0, 0)] * (values.ndim - 1)
    return jnp.pad(values, padding)[offset:]


def pick_dot(left_side, weights, first_mode):
    first_part = jnp.dot(left_side, weights[0], preferred_element_type=jnp.float32)
    second_part = jnp.dot(left_side, weights[1], preferred_element_type=jnp.float32)
    return jnp.where(first_mode, first_part, second_part)


def pick_back(gradient, weights, first_mode):
    dims = (((1,), (1,)), ((), ()))
    first_part = lax.dot_general(gradient, weights[0], dims, preferred_element_type=jnp.float32)
    second_part = lax.dot_general(gradient, weights[1], dims, preferred_element_type=jnp.float32)
    return jnp.where(first_mode, first_part, second_part)


def weight_grads(left_side, gradient, first_mode):
    nothing = jnp.zeros_like(gradient)
    dims = (((0,), (0,)), ((), ()))
    first_part = lax.dot_general(
        left_side,
        jnp.where(first_mode, gradient, nothing),
        dims,
        preferred_element_type=jnp.float32,
    )
    second_part = lax.dot_general(
        left_side,
        jnp.where(first_mode, nothing, gradient),
        dims,
        preferred_element_type=jnp.float32,
    )
    return jnp.stack([first_part, second_part])


def finish_rows(normed_grad, hidden, inverse, cotan, norm_gain):
    scaled = normed_grad * norm_gain
    gain_terms = jnp.sum(normed_grad * hidden * inverse, axis=0)
    cubed = inverse * inverse * inverse
    rows = (
        cotan + inverse * scaled - hidden * cubed * jnp.mean(scaled * hidden, axis=1, keepdims=True)
    )
    return (rows.astype(jnp.bfloat16), gain_terms)


def shards(
    hidden_in,
    segment_ids,
    modality,
    norm_gain,
    in_proj,
    conv_weight,
    conv_bias,
    x_proj,
    dt_proj,
    dt_bias,
    a_log,
    skip_gain,
    out_proj,
    out_grad,
):
    tokens = hidden_in.shape[0]
    model_width = hidden_in.shape[1]
    channels = conv_weight.shape[1]
    conv_taps = conv_weight.shape[0]
    rank_dim = dt_proj.shape[1]
    state_dim = a_log.shape[0]
    block_len = 32
    block_count = tokens // block_len
    first_mode = (modality == 0)[:, None]
    hidden = hidden_in.astype(jnp.float32)
    inverse = lax.rsqrt(jnp.mean(hidden * hidden, axis=1, keepdims=True) + EPS)
    normed_b = (hidden * inverse * norm_gain).astype(jnp.bfloat16)
    in_wide = in_proj.reshape(2, model_width, 2 * channels)
    both_parts = pick_dot(normed_b, in_wide, first_mode)
    inner_x = both_parts[:, :channels]
    gate_z = both_parts[:, channels:]
    same_doc = [jnp.ones((tokens, 1), jnp.float32)]
    for offset in range(1, conv_taps):
        earlier_seg = jnp.pad(segment_ids, (offset, 0), constant_values=-1)[:tokens]
        same_doc.append((earlier_seg == segment_ids).astype(jnp.float32)[:, None])
    conv_sum = conv_bias + conv_weight[conv_taps - 1] * inner_x
    for offset in range(1, conv_taps):
        conv_sum = (
            conv_sum
            + conv_weight[conv_taps - 1 - offset] * lagged(inner_x, offset) * same_doc[offset]
        )
    activated_b = jax.nn.silu(conv_sum).astype(jnp.bfloat16)
    activated = activated_b.astype(jnp.float32)
    projected = lax.psum(pick_dot(activated_b, x_proj, first_mode), "tensor")
    rank_b = projected[:, :rank_dim].astype(jnp.bfloat16)
    b_coeff = projected[:, rank_dim : rank_dim + state_dim]
    c_coeff = projected[:, rank_dim + state_dim :]
    step_pre = pick_dot(rank_b, dt_proj, first_mode) + jnp.where(first_mode, dt_bias[0], dt_bias[1])
    step_size = jax.nn.softplus(step_pre)
    decay = -jnp.exp(a_log)
    keep_mask = same_doc[1][:, 0]
    position = jnp.arange(block_len)
    ordered = position[:, None] >= position[None, :]

    def split_blocks(values):
        return values.reshape((block_count, block_len) + values.shape[1:])

    def block_terms(step_blk, act_blk, b_blk, keep_blk):
        log_factor = step_blk[:, None, :] * decay[None]
        factor = jnp.exp(log_factor) * keep_blk[:, None, None]
        source = (step_blk * act_blk)[:, None, :] * b_blk[:, :, None]
        running = jnp.cumsum(log_factor, axis=0)
        resets = jnp.cumsum(1.0 - keep_blk)
        linked = (resets[:, None] == resets[None, :]) & ordered
        spread = jnp.minimum(running[:, None] - running[None, :], 0.0)
        weights = jnp.where(linked[:, :, None, None], jnp.exp(spread), 0.0)
        from_start = jnp.where((resets == 0.0)[:, None, None], jnp.exp(running), 0.0)
        return (factor, source, weights, from_start)

    def block_states(source, weights, from_start, start_state):
        return jnp.sum(weights * source[None], axis=1) + from_start * start_state[None]

    def forward_block(start_state, inputs):
        step_blk, act_blk, b_blk, c_blk, keep_blk = inputs
        factor, source, weights, from_start = block_terms(step_blk, act_blk, b_blk, keep_blk)
        states = block_states(source, weights, from_start, start_state)
        emitted = jnp.sum(c_blk[:, :, None] * states, axis=1)
        return (states[-1], (emitted, start_state))

    scan_inputs = (
        split_blocks(step_size),
        split_blocks(activated),
        split_blocks(b_coeff),
        split_blocks(c_coeff),
        split_blocks(keep_mask),
    )
    _, (scanned, starts) = lax.scan(
        forward_block, jnp.zeros((state_dim, channels), jnp.float32), scan_inputs
    )
    scanned = scanned.reshape(tokens, channels)
    sig_z = jax.nn.sigmoid(gate_z)
    silu_z = gate_z * sig_z
    mixed_out = scanned + skip_gain * activated
    gated_b = (mixed_out * silu_z).astype(jnp.bfloat16)
    partial_out = pick_dot(gated_b, out_proj, first_mode)
    output = (hidden + lax.psum(partial_out, "tensor")).astype(jnp.bfloat16)
    cotan = out_grad.astype(jnp.float32)
    out_proj_grad = weight_grads(gated_b, out_grad, first_mode)
    gated_grad = pick_back(out_grad, out_proj, first_mode)
    mixed_grad = gated_grad * silu_z
    gate_grad = gated_grad * mixed_out * sig_z * (1.0 + gate_z * (1.0 - sig_z))
    skip_grad = jnp.sum(mixed_grad * activated, axis=0)

    def backward_block(carried, inputs):
        later_term, rate_grad = carried
        step_blk, act_blk, b_blk, c_blk, keep_blk, dy_blk, start_state = inputs
        factor, source, weights, from_start = block_terms(step_blk, act_blk, b_blk, keep_blk)
        states = block_states(source, weights, from_start, start_state)
        emitted = c_blk[:, :, None] * dy_blk[:, None, :]
        emitted = emitted.at[-1].add(later_term)
        dstate = jnp.sum(weights * emitted[:, None], axis=0)
        log_grad = dstate * (states - source)
        weighted = jnp.sum(dstate * b_blk[:, :, None], axis=1)
        step_grad = weighted * act_blk + jnp.sum(log_grad * decay[None], axis=1)
        act_grad = weighted * step_blk
        b_grad = jnp.sum(dstate * (step_blk * act_blk)[:, None, :], axis=2)
        c_grad = jnp.sum(dy_blk[:, None, :] * states, axis=2)
        rate_grad = rate_grad + jnp.sum(log_grad * step_blk[:, None, :], axis=0)
        return ((factor[0] * dstate[0], rate_grad), (step_grad, act_grad, b_grad, c_grad))

    zero_state = jnp.zeros((state_dim, channels), jnp.float32)
    (_, rate_grad), (step_grad, scan_act_grad, b_grad, c_grad) = lax.scan(
        backward_block,
        (zero_state, zero_state),
        scan_inputs + (split_blocks(mixed_grad), starts),
        reverse=True,
    )
    step_grad = step_grad.reshape(tokens, channels)
    scan_act_grad = scan_act_grad.reshape(tokens, channels)
    b_grad = b_grad.reshape(tokens, state_dim)
    c_grad = c_grad.reshape(tokens, state_dim)
    a_log_grad = rate_grad * decay
    pre_grad_b = (step_grad * jax.nn.sigmoid(step_pre)).astype(jnp.bfloat16)
    pre_grad = pre_grad_b.astype(jnp.float32)
    dt_bias_grad = jnp.stack(
        [
            jnp.sum(jnp.where(first_mode, pre_grad, 0.0), axis=0),
            jnp.sum(jnp.where(first_mode, 0.0, pre_grad), axis=0),
        ]
    )
    dt_proj_grad = weight_grads(rank_b, pre_grad_b, first_mode)
    rank_part = pick_back(pre_grad_b, dt_proj, first_mode)
    proj_grad = lax.psum(jnp.concatenate([rank_part, b_grad, c_grad], axis=1), "tensor")
    proj_grad_b = proj_grad.astype(jnp.bfloat16)
    x_proj_grad = weight_grads(activated_b, proj_grad_b, first_mode)
    act_grad = mixed_grad * skip_gain + scan_act_grad + pick_back(proj_grad_b, x_proj, first_mode)
    sig_conv = jax.nn.sigmoid(conv_sum)
    conv_grad = act_grad * sig_conv * (1.0 + conv_sum * (1.0 - sig_conv))
    conv_bias_grad = jnp.sum(conv_grad, axis=0)
    weight_rows = []
    x_grad = jnp.zeros_like(inner_x)
    for tap_index in range(conv_taps):
        offset = conv_taps - 1 - tap_index
        masked = conv_grad * same_doc[offset]
        weight_rows.append(jnp.sum(masked * lagged(inner_x, offset), axis=0))
        x_grad = x_grad + conv_weight[tap_index] * leading(masked, offset)
    conv_weight_grad = jnp.stack(weight_rows)
    both_grad_b = jnp.concatenate([x_grad, gate_grad], axis=1).astype(jnp.bfloat16)
    in_proj_grad = weight_grads(normed_b, both_grad_b, first_mode).reshape(
        2, model_width, 2, channels
    )
    normed_part = pick_back(both_grad_b, in_wide, first_mode)
    normed_grad = lax.psum(normed_part, "tensor")
    input_grad, norm_gain_grad = finish_rows(normed_grad, hidden, inverse, cotan, norm_gain)
    shares = (
        lax.psum_scatter(norm_gain_grad, "dp", scatter_dimension=0, tiled=True),
        lax.psum_scatter(in_proj_grad, "dp", scatter_dimension=1, tiled=True),
        lax.psum_scatter(conv_weight_grad, "dp", scatter_dimension=1, tiled=True),
        lax.psum_scatter(conv_bias_grad, "dp", scatter_dimension=0, tiled=True),
        lax.psum_scatter(x_proj_grad, "dp", scatter_dimension=1, tiled=True),
        lax.psum_scatter(dt_proj_grad, "dp", scatter_dimension=2, tiled=True),
        lax.psum_scatter(dt_bias_grad, "dp", scatter_dimension=1, tiled=True),
        lax.psum_scatter(a_log_grad, "dp", scatter_dimension=1, tiled=True),
        lax.psum_scatter(skip_grad, "dp", scatter_dimension=0, tiled=True),
        lax.psum_scatter(out_proj_grad, "dp", scatter_dimension=2, tiled=True),
    )
    summed = (
        lax.all_gather(shares[0], "dp", axis=0, tiled=True),
        lax.all_gather(shares[1], "dp", axis=1, tiled=True),
        lax.all_gather(shares[2], "dp", axis=1, tiled=True),
        lax.all_gather(shares[3], "dp", axis=0, tiled=True),
        lax.all_gather(shares[4], "dp", axis=1, tiled=True),
        lax.all_gather(shares[5], "dp", axis=2, tiled=True),
        lax.all_gather(shares[6], "dp", axis=1, tiled=True),
        lax.all_gather(shares[7], "dp", axis=1, tiled=True),
        lax.all_gather(shares[8], "dp", axis=0, tiled=True),
        lax.all_gather(shares[9], "dp", axis=2, tiled=True),
    )
    return (
        output,
        input_grad,
        summed[0],
        summed[1],
        summed[2],
        summed[3],
        summed[4],
        summed[5],
        summed[6],
        summed[7],
        summed[8],
        summed[9],
    )


def solution(mesh):
    in_specs = (
        P("dp", None),
        P("dp"),
        P("dp"),
        P(),
        P(None, None, None, "tensor"),
        P(None, "tensor"),
        P("tensor"),
        P(None, "tensor", None),
        P(None, None, "tensor"),
        P(None, "tensor"),
        P(None, "tensor"),
        P("tensor"),
        P(None, "tensor", None),
        P("dp", None),
    )
    out_specs = (
        P("dp", None),
        P("dp", None),
        P(),
        P(None, None, None, "tensor"),
        P(None, "tensor"),
        P("tensor"),
        P(None, "tensor", None),
        P(None, None, "tensor"),
        P(None, "tensor"),
        P(None, "tensor"),
        P("tensor"),
        P(None, "tensor", None),
    )
    return jax.shard_map(shards, mesh=mesh, in_specs=in_specs, out_specs=out_specs, check_vma=False)
```

profile of v0, /device:TPU:0, one launch (start us, length us, event | category | flops | bytes accessed | tf_op | source)
XLA Modules:
  0.0 3215.8 jit_solution(3848984042884975198)
XLA Ops:
  88.3 38.5 %all-reduce.18.cloned.1.call-done = f32[768,160]{0,1:T(8,128)} async-done(((f32[768,160]{0,1:T(8,128)}), f32[768,160]{0,1:T(8,128)}) %all-reduce.18.cloned.1.call-update) | async-done | bytes 491536 | tf_op jit(solution)/shard_map/psum | solution.py:104
  137.3 665.2 %while.41 = (s32[]{:T(128)}, f32[16,1024]{1,0:T(8,128)S(1)}, f32[24,32,1024]{2,1,0:T(8,128)}, f32[24,16,1024]{2,1,0:T(8,128)}, f32[24,32]{1,0:T(8,128)S(1)}, /*i...) while((s32[]{:T(128)}, f32[16,1024]{1,0:T(8,128)S(1)}, ...), condition=%wide.region_7.8_spmd.clone, body=%wide.region_2.7_spmd.clone.sunk | while | flops 103288864 | bytes 18501096 | solution.py:147
  808.2 1080.5 %while.42 = (s32[]{:T(128)}, f32[16,1024]{1,0:T(8,128)S(1)}, f32[16,1024]{1,0:T(8,128)S(1)}, f32[24,32,1024]{2,1,0:T(8,128)}, f32[24,32,1024]{2,1,0:T(8,128)}, /...) while((s32[]{:T(128)}, f32[16,1024]{1,0:T(8,128)S(1)}, ...), condition=%wide.region_19.20_spmd.clone, body=%wide.region_9.19_spmd.clone.sunk | while | flops 143264800 | bytes 28964544 | solution.py:182
  816.5 28.1 multiply_reduce_fusion.20
  861.5 28.1 multiply_reduce_fusion.20
  951.6 28.1 multiply_reduce_fusion.20
  1041.6 28.1 multiply_reduce_fusion.20
  1086.6 28.1 multiply_reduce_fusion.20
  1176.7 28.1 multiply_reduce_fusion.20
  1221.7 28.1 multiply_reduce_fusion.20
  1266.7 28.1 multiply_reduce_fusion.20
  1311.7 28.1 multiply_reduce_fusion.20
  1356.8 28.1 multiply_reduce_fusion.20
  1401.8 28.1 multiply_reduce_fusion.20
  1446.8 28.1 multiply_reduce_fusion.20
  1536.8 28.1 multiply_reduce_fusion.20
  1626.8 28.1 multiply_reduce_fusion.20
  1671.9 28.1 multiply_reduce_fusion.20
  2075.1 43.0 %reshape.370 = f32[2048,4096]{1,0:T(8,128)} reshape(f32[2048,2,2,1024]{3,2,1,0:T(2,128)} %copy_bitcast_fusion) | data formatting | bytes 67108864
  2170.5 152.6 %reduce-scatter.23.cloned.1.call-done = f32[256,4096]{1,0:T(8,128)} async-done(((f32[2048,4096]{1,0:T(8,128)}), f32[256,4096]{1,0:T(8,128)}) %reduce-scatter.23.cloned.1.call-update) | async-done | bytes 4194320
  2369.9 28.4 reduce-scatter.25.cloned.1.call-done
  2485.5 430.8 %all-reduce.20.cloned.1.call-done = (f32[768,2048]{1,0:T(8,128)}, f32[768,2048]{1,0:T(8,128)}) async-done(((f32[768,2048]{1,0:T(8,128)}, f32[768,2048]{1,0:T(8,128)}), (f32[768,2048]{1,0:T(8,128)}, f32[768,2048]{1,0:T(8,128)})) %all-reduce.20.cloned.1.call-update) | async-done | bytes 12582928 | tf_op jit(solution)/shard_map/psum | solution.py:156
  2978.1 32.4 %all-gather.14.cloned.1.call-done = f32[2,1024,2048]{2,1,0:T(8,128)} async-done(((f32[2,1024,256]{2,1,0:T(8,128)}), f32[2,1024,2048]{2,1,0:T(8,128)}) %all-gather.14.cloned.1.call-update) | async-done | bytes 16777232 | tf_op jit(solution)/shard_map/all_gather | solution.py:247
  3010.5 162.9 %all-gather.8.cloned.1.call-done = f32[2,2048,2,1024]{3,2,1,0:T(2,128)} async-done(((f32[2,256,2,1024]{3,2,1,0:T(2,128)}), f32[2,2048,2,1024]{3,2,1,0:T(2,128)}) %all-gather.8.cloned.1.call-update) | async-done | bytes 33554448 | tf_op jit(solution)/shard_map/all_gather | solution.py:239
  (1214 shorter events, 1886.2 us)
Async XLA Ops:
  7.2 119.6 %all-reduce.18.cloned.1.call-start = ((), (), s32[]{:S(2)}) async-start(), calls=%async_computation.7 | async-start | bytes 983040 | tf_op jit(solution)/shard_map/psum | solution.py:104
  43.2 28.1 copy-start.42
  43.2 28.1 copy-start.44
  43.2 42.9 %copy-start.28 = (f32[768]{0:T(1024)}, f32[768]{0:T(1024)S(1)}, u32[]{:S(2)}) copy-start(f32[768]{0:T(1024)S(1)} %get-tuple-element.691) | copy-start | bytes 9220
  86.0 42.7 %copy-start.15 = (bf16[2,128,1024]{2,1,0:T(8,128)(2,1)S(1)}, bf16[2,128,1024]{2,1,0:T(8,128)(2,1)}, u32[]{:S(2)}) copy-start(bf16[2,128,1024]{2,1,0:T(8,128)(2,1)} %param.28) | copy-start | bytes 1572868
  86.0 2035.2 %reduce-scatter.17.cloned.1.call-start = ((), (), s32[]{:S(2)}) async-start(), calls=%async_computation.11 | async-start | bytes 1179648 | tf_op jit(solution)/shard_map/reduce_scatter | solution.py:231
  1895.8 32.6 %copy-start.1 = (bf16[768,1024]{1,0:T(8,128)(2,1)S(1)}, bf16[768,1024]{1,0:T(8,128)(2,1)}, u32[]{:S(2)}) copy-start(bf16[768,1024]{1,0:T(8,128)(2,1)} %copy-done) | copy-start | bytes 4718596
  1895.8 248.3 %reduce-scatter.15.cloned.1.call-start = ((), (), s32[]{:S(2)}) async-start(), calls=%async_computation.9 | async-start | bytes 1474560 | tf_op jit(solution)/shard_map/reduce_scatter | solution.py:230
  1932.7 236.9 %reduce-scatter.21.cloned.1.call-start = ((), (), s32[]{:S(2)}) async-start(), calls=%async_computation.14 | async-start | bytes 18874368 | tf_op jit(solution)/shard_map/reduce_scatter | solution.py:235
  1967.7 355.4 %reduce-scatter.23.cloned.1.call-start = ((), (), s32[]{:S(2)}) async-start(), calls=%async_computation.16 | async-start | bytes 37748736
  2118.1 242.1 %reduce-scatter.27.cloned.1.call-start = ((), (), s32[]{:S(2)}) async-start(), calls=%async_computation.18 | async-start | bytes 589824
  2119.3 279.0 %reduce-scatter.25.cloned.1.call-start = ((), (), s32[]{:S(2)}) async-start(), calls=%async_computation.17 | async-start | bytes 589824
  2120.4 312.9 %reduce-scatter.19.cloned.1.call-start = ((), (), s32[]{:S(2)}) async-start(), calls=%async_computation.13 | async-start | bytes 73728 | tf_op jit(solution)/shard_map/reduce_scatter | solution.py:233
  2121.1 337.8 %all-gather.12.cloned.1.call-start = ((), (), s32[]{:S(2)}) async-start(), calls=%async_computation.12 | async-start | bytes 1179648 | tf_op jit(solution)/shard_map/all_gather | solution.py:243
  2121.9 363.7 %all-gather.10.cloned.1.call-start = ((), (), s32[]{:S(2)}) async-start(), calls=%async_computation.10 | async-start | bytes 1474560 | tf_op jit(solution)/shard_map/all_gather | solution.py:242
  2144.2 772.1 %all-reduce.20.cloned.1.call-start = ((), (), s32[]{:S(2)}) async-start(), calls=%async_computation.19 | async-start | bytes 25165824 | tf_op jit(solution)/shard_map/psum | solution.py:156
  2169.6 840.9 %all-gather.14.cloned.1.call-start = ((), (), s32[]{:S(2)}) async-start(), calls=%async_computation.15 | async-start | bytes 18874368 | tf_op jit(solution)/shard_map/all_gather | solution.py:247
  2170.2 1003.2 %all-gather.8.cloned.1.call-start = ((), (), s32[]{:S(2)}) async-start(), calls=%async_computation.8 | async-start | bytes 37748736 | tf_op jit(solution)/shard_map/all_gather | solution.py:239
  2916.3 53.2 %copy-start.26 = (f32[768]{0:T(1024)S(1)}, f32[768]{0:T(1024)}, u32[]{:S(2)}) copy-start(f32[768]{0:T(1024)} %get-tuple-element.689) | copy-start | bytes 9220
  3173.4 29.3 slice-start
  3174.0 24.5 copy-start.14
  3174.0 28.7 slice-start.1
  3174.0 28.7 slice-start.2
  3174.0 28.7 slice-start.3
  (48 other events, 297.4 us)
Sparse Core Ops, SparseCore 0:
  86.1 40.5 all-reduce.17
  1896.0 35.8 reduce-scatter.16
  1936.0 37.2 reduce-scatter.14
  1977.1 115.9 reduce-scatter.20
  2118.2 204.7 reduce-scatter.22
  2326.0 34.1 reduce-scatter.26
  2364.1 34.0 reduce-scatter.24
  2401.8 31.3 reduce-scatter.18
  2435.3 23.5 all-gather.11
  2460.8 24.7 all-gather.9
  2489.5 426.7 all-reduce.19
  2918.2 92.2 all-gather.13
  3012.5 160.7 all-gather.7
where the time goes:
time: 3240 us; the launch traced here: 3220 us
  other arithmetic  1630 us (50%)
  waiting for transfers between devices  938 us (29%)
  local copies, waits for them, and re-layouts  369 us (11%)
  matrix products  154 us (5%)
  blocking collectives  102 us (3%)
    reduce_sum x48, other arithmetic, block_states(): jnp.sum(weights * source[None], axis=1) + from_start * start_state[None]  1170 us
    psum x1, waiting for transfers between devices, shards(): output = (hidden + lax.psum(partial_out, 'tensor')).astype(jnp.bfloat16)  431 us
    unnamed x16, waiting for transfers between devices  205 us
    all_gather x1, waiting for transfers between devices, shards(): lax.all_gather(shares[1], 'dp', axis=1, tiled=True)  163 us
    unnamed x142, local copies, waits for them, and re-layouts  122 us
    mul x96, other arithmetic, block_terms(): source = (step_blk * act_blk)[:, None, :] * b_blk[:, :, None]  122 us
    reduce_sum x24, other arithmetic, backward_block(): step_grad = weighted * act_blk + jnp.sum(log_grad * decay[None], axis=1)  93.5 us
  transfers between devices with their start and end apart: 13, of which 10 were waited for; matrix products, arithmetic and copies ran while one was open for 9% of the time, Pallas kernels for 0%

commit v1 on v0

--- a/solution.py
+++ b/solution.py
@@ -4,6 +4,19 @@
 from jax.sharding import PartitionSpec as P
 
 EPS = 1e-05
+
+
+def collect(x, axis, dim):
+    size, index, span = (lax.axis_size(axis), lax.axis_index(axis), x.shape[dim])
+    right = [(i, (i + 1) % size) for i in range(size)]
+    filled = jnp.zeros((*x.shape[:dim], size * span, *x.shape[dim + 1 :]), x.dtype)
+    held = x
+    for lap in range(size):
+        source = (index - lap) % size
+        filled = lax.dynamic_update_slice_in_dim(filled, held, source * span, axis=dim)
+        if lap < size - 1:
+            held = lax.ppermute(held, axis, right)
+    return filled
 
 
 def lagged(values, offset):
@@ -236,7 +249,7 @@
     )
     summed = (
         lax.all_gather(shares[0], "dp", axis=0, tiled=True),
-        lax.all_gather(shares[1], "dp", axis=1, tiled=True),
+        collect(shares[1], "dp", 1),
         lax.all_gather(shares[2], "dp", axis=1, tiled=True),
         lax.all_gather(shares[3], "dp", axis=0, tiled=True),
         lax.all_gather(shares[4], "dp", axis=1, tiled=True),

time: 3240 us -> 3020 us (0.932)
  waiting for transfers between devices: 938 us -> 680 us
  blocking collectives: 102 us -> 183 us
  other arithmetic: 1630 us -> 1560 us
    ppermute x0 -> x7, waiting for transfers between devices: none -> 256 us  [collect(): held = lax.ppermute(held, axis, right)]
    psum x1, waiting for transfers between devices: 431 us -> 200 us  [shards(): output = (hidden + lax.psum(partial_out, 'tensor')).astype(jnp.bfloat16)]
    all_gather x1 -> x0, waiting for transfers between devices: 163 us -> none  [shards(): lax.all_gather(shares[1], 'dp', axis=1, tiled=True)]
    unnamed x16 -> x15, waiting for transfers between devices: 205 us -> 154 us
    all_gather x1, blocking collectives: 8.84 us -> 51.7 us  [shards(): lax.all_gather(shares[2], 'dp', axis=1, tiled=True)]
    all_gather x1, blocking collectives: 8.83 us -> 47.2 us  [shards(): lax.all_gather(shares[6], 'dp', axis=1, tiled=True)]
    reduce_sum x48, other arithmetic: 1170 us -> 1130 us  [block_states(): jnp.sum(weights * source[None], axis=1) + from_start * start_state[None]]
    dynamic_update_slice x0 -> x7, local copies, waits for them, and re-layouts: none -> 33.5 us  [collect(): lax.dynamic_update_slice_in_dim(filled, held, source * span, axis=dim)]
  transfers between devices with their start and end apart: 13 -> 19, of which waited for: 10 -> 9; matrix products, arithmetic and copies ran while one was open for 9% -> 10% of each run, Pallas kernels for 0% -> 0%
where the time goes in v1:
time: 3020 us; the launch traced here: 3000 us
  other arithmetic  1560 us (52%)
  waiting for transfers between devices  680 us (23%)
  local copies, waits for them, and re-layouts  398 us (13%)
  blocking collectives  183 us (6%)
  matrix products  155 us (5%)
    reduce_sum x48, other arithmetic, block_states(): jnp.sum(weights * source[None], axis=1) + from_start * start_state[None]  1130 us
    ppermute x7, waiting for transfers between devices, collect(): held = lax.ppermute(held, axis, right)  256 us
    psum x1, waiting for transfers between devices, shards(): output = (hidden + lax.psum(partial_out, 'tensor')).astype(jnp.bfloat16)  200 us
    unnamed x15, waiting for transfers between devices  154 us
    unnamed x157, local copies, waits for them, and re-layouts  105 us
    reduce_sum x24, other arithmetic, backward_block(): step_grad = weighted * act_blk + jnp.sum(log_grad * decay[None], axis=1)  93.9 us
    mul x96, other arithmetic, block_terms(): source = (step_blk * act_blk)[:, None, :] * b_blk[:, :, None]  88.6 us
  transfers between devices with their start and end apart: 19, of which 9 were waited for; matrix products, arithmetic and copies ran while one was open for 10% of the time, Pallas kernels for 0%

profile of v1, /device:TPU:0, one launch (start us, length us, event | category | flops | bytes accessed | tf_op | source)
XLA Modules:
  0.0 3001.3 jit_solution(7988131500904008131)
XLA Ops:
  91.5 38.5 %all-reduce.18.cloned.1.call-done = f32[768,160]{0,1:T(8,128)} async-done(((f32[768,160]{0,1:T(8,128)}), f32[768,160]{0,1:T(8,128)}) %all-reduce.18.cloned.1.call-update) | async-done | bytes 491536 | tf_op jit(solution)/shard_map/psum | solution.py:117
  140.4 599.0 %while.41 = (s32[]{:T(128)}, f32[16,1024]{1,0:T(8,128)S(1)}, f32[24,32,1024]{2,1,0:T(8,128)}, f32[24,16,1024]{2,1,0:T(8,128)}, f32[24,32]{1,0:T(8,128)S(1)}, /*i...) while((s32[]{:T(128)}, f32[16,1024]{1,0:T(8,128)S(1)}, ...), condition=%wide.region_7.8_spmd.clone, body=%wide.region_2.7_spmd.clone.sunk | while | flops 103288864 | bytes 18501096 | solution.py:160
  745.0 1076.5 %while.42 = (s32[]{:T(128)}, f32[16,1024]{1,0:T(8,128)S(1)}, f32[16,1024]{1,0:T(8,128)S(1)}, f32[24,32,1024]{2,1,0:T(8,128)}, f32[24,32,1024]{2,1,0:T(8,128)}, /...) while((s32[]{:T(128)}, f32[16,1024]{1,0:T(8,128)S(1)}, ...), condition=%wide.region_19.20_spmd.clone, body=%wide.region_9.19_spmd.clone.sunk | while | flops 143264800 | bytes 28964544 | solution.py:195
  754.0 28.1 multiply_reduce_fusion.20
  798.9 28.1 multiply_reduce_fusion.20
  843.7 28.1 multiply_reduce_fusion.20
  888.6 28.1 multiply_reduce_fusion.20
  933.4 28.1 multiply_reduce_fusion.20
  978.3 28.1 multiply_reduce_fusion.20
  1023.1 28.1 multiply_reduce_fusion.20
  1292.3 28.1 multiply_reduce_fusion.20
  1337.1 28.1 multiply_reduce_fusion.20
  1740.8 28.1 multiply_reduce_fusion.20
  2008.1 43.1 %reshape.370 = f32[2048,4096]{1,0:T(8,128)} reshape(f32[2048,2,2,1024]{3,2,1,0:T(2,128)} %copy_bitcast_fusion) | data formatting | bytes 67108864
  2103.3 152.8 %reduce-scatter.23.cloned.1.call-done = f32[256,4096]{1,0:T(8,128)} async-done(((f32[2048,4096]{1,0:T(8,128)}), f32[256,4096]{1,0:T(8,128)}) %reduce-scatter.23.cloned.1.call-update) | async-done | bytes 4194320
  2279.4 51.0 %collective-permute-done = f32[2,256,2,1024]{3,2,1,0:T(2,128)S(1)} collective-permute-done((f32[2,256,2,1024]{3,2,1,0:T(2,128)S(1)}, f32[2,256,2,1024]{3,2,1,0:T(2,128)S(1)}, u32[]{:S(2)}, u32[]{:S(2)}) %collective-permute-start) | collective-permute-done | bytes 4194336 | tf_op jit(solution)/shard_map/ppermute | solution.py:18
  2332.4 50.5 %collective-permute-done.1 = f32[2,256,2,1024]{3,2,1,0:T(2,128)S(1)} collective-permute-done((f32[2,256,2,1024]{3,2,1,0:T(2,128)S(1)}, f32[2,256,2,1024]{3,2,1,0:T(2,128)S(1)}, u32[]{:S(2)}, u32[]{:S(2)}) %collective-permute-start.1) | collective-permute-done | bytes 4194336 | tf_op jit(solution)/shard_map/ppermute | solution.py:18
  2385.0 56.9 %collective-permute-done.2 = f32[2,256,2,1024]{3,2,1,0:T(2,128)S(1)} collective-permute-done((f32[2,256,2,1024]{3,2,1,0:T(2,128)S(1)}, f32[2,256,2,1024]{3,2,1,0:T(2,128)S(1)}, u32[]{:S(2)}, u32[]{:S(2)}) %collective-permute-start.2) | collective-permute-done | bytes 4194336 | tf_op jit(solution)/shard_map/ppermute | solution.py:18
  2443.8 48.8 %collective-permute-done.3 = f32[2,256,2,1024]{3,2,1,0:T(2,128)S(1)} collective-permute-done((f32[2,256,2,1024]{3,2,1,0:T(2,128)S(1)}, f32[2,256,2,1024]{3,2,1,0:T(2,128)S(1)}, u32[]{:S(2)}, u32[]{:S(2)}) %collective-permute-start.3) | collective-permute-done | bytes 4194336 | tf_op jit(solution)/shard_map/ppermute | solution.py:18
  2494.6 48.9 %collective-permute-done.4 = f32[2,256,2,1024]{3,2,1,0:T(2,128)} collective-permute-done((f32[2,256,2,1024]{3,2,1,0:T(2,128)S(1)}, f32[2,256,2,1024]{3,2,1,0:T(2,128)}, u32[]{:S(2)}, u32[]{:S(2)}) %collective-permute-start.4) | collective-permute-done | bytes 4194336 | tf_op jit(solution)/shard_map/ppermute | solution.py:18
  2546.4 47.2 %all_gather.32 = f32[2,1024]{1,0:T(2,128)S(1)} all-gather(f32[2,128]{1,0:T(2,128)S(1)} %copy.76), channel_id=1, replica_groups=mesh['dp'=8,'tensor'=4] {'dp'}, dimensions={1}, use_global_device_ids=true | all-gather | bytes 9216 | tf_op jit(solution)/shard_map/all_gather | solution.py:257
  2594.8 51.7 %all_gather.28 = f32[4,1024]{1,0:T(4,128)S(1)} all-gather(f32[4,128]{1,0:T(4,128)S(1)} %copy.74), channel_id=1, replica_groups=mesh['dp'=8,'tensor'=4] {'dp'}, dimensions={1}, use_global_device_ids=true | all-gather | bytes 18432 | tf_op jit(solution)/shard_map/all_gather | solution.py:253
  2654.8 199.7 %all-reduce.20.cloned.1.call-done = (f32[768,2048]{1,0:T(8,128)}, f32[768,2048]{1,0:T(8,128)}) async-done(((f32[768,2048]{1,0:T(8,128)}, f32[768,2048]{1,0:T(8,128)}), (f32[768,2048]{1,0:T(8,128)}, f32[768,2048]{1,0:T(8,128)})) %all-reduce.20.cloned.1.call-update) | async-done | bytes 12582928 | tf_op jit(solution)/shard_map/psum | solution.py:169
  2916.4 32.2 %all-gather.11.cloned.1.call-done = f32[2,1024,2048]{2,1,0:T(8,128)} async-done(((f32[2,1024,256]{2,1,0:T(8,128)}), f32[2,1024,2048]{2,1,0:T(8,128)}) %all-gather.11.cloned.1.call-update) | async-done | bytes 16777232 | tf_op jit(solution)/shard_map/all_gather | solution.py:260
  (1248 shorter events, 1879.9 us)
Async XLA Ops:
  7.2 122.7 %all-reduce.18.cloned.1.call-start = ((), (), s32[]{:S(2)}) async-start(), calls=%async_computation.7 | async-start | bytes 983040 | tf_op jit(solution)/shard_map/psum | solution.py:117
  10.4 64.0 %copy-start.38 = (f32[1,1024]{1,0:T(1,128)}, f32[1,1024]{1,0:T(1,128)S(1)}, u32[]{:S(2)}) copy-start(f32[1,1024]{1,0:T(1,128)S(1)} %get-tuple-element.685) | copy-start | bytes 12292
  10.4 64.0 %copy-start.40 = (f32[1,1024]{1,0:T(1,128)}, f32[1,1024]{1,0:T(1,128)S(1)}, u32[]{:S(2)}) copy-start(f32[1,1024]{1,0:T(1,128)S(1)} %get-tuple-element.686) | copy-start | bytes 12292
  10.5 64.0 %copy-start.42 = (f32[1,1024]{1,0:T(1,128)}, f32[1,1024]{1,0:T(1,128)S(1)}, u32[]{:S(2)}) copy-start(f32[1,1024]{1,0:T(1,128)S(1)} %get-tuple-element.687) | copy-start | bytes 12292
  10.5 64.0 %copy-start.44 = (f32[1,1024]{1,0:T(1,128)}, f32[1,1024]{1,0:T(1,128)S(1)}, u32[]{:S(2)}) copy-start(f32[1,1024]{1,0:T(1,128)S(1)} %get-tuple-element.688) | copy-start | bytes 12292
  89.2 1965.1 %reduce-scatter.17.cloned.1.call-start = ((), (), s32[]{:S(2)}) async-start(), calls=%async_computation.10 | async-start | bytes 1179648 | tf_op jit(solution)/shard_map/reduce_scatter | solution.py:244
  1828.7 248.5 %reduce-scatter.15.cloned.1.call-start = ((), (), s32[]{:S(2)}) async-start(), calls=%async_computation.8 | async-start | bytes 1474560 | tf_op jit(solution)/shard_map/reduce_scatter | solution.py:243
  1865.7 237.3 %reduce-scatter.21.cloned.1.call-start = ((), (), s32[]{:S(2)}) async-start(), calls=%async_computation.13 | async-start | bytes 18874368 | tf_op jit(solution)/shard_map/reduce_scatter | solution.py:248
  1900.6 355.5 %reduce-scatter.23.cloned.1.call-start = ((), (), s32[]{:S(2)}) async-start(), calls=%async_computation.15 | async-start | bytes 37748736
  2051.2 494.3 %reduce-scatter.27.cloned.1.call-start = ((), (), s32[]{:S(2)}) async-start(), calls=%async_computation.17 | async-start | bytes 589824
  2052.4 541.2 %reduce-scatter.25.cloned.1.call-start = ((), (), s32[]{:S(2)}) async-start(), calls=%async_computation.16 | async-start | bytes 589824
  2053.5 593.0 %reduce-scatter.19.cloned.1.call-start = ((), (), s32[]{:S(2)}) async-start(), calls=%async_computation.12 | async-start | bytes 73728 | tf_op jit(solution)/shard_map/reduce_scatter | solution.py:246
  2054.3 600.5 %all-gather.9.cloned.1.call-start = ((), (), s32[]{:S(2)}) async-start(), calls=%async_computation.11 | async-start | bytes 1179648 | tf_op jit(solution)/shard_map/all_gather | solution.py:256
  2055.0 599.8 %all-gather.7.cloned.1.call-start = ((), (), s32[]{:S(2)}) async-start(), calls=%async_computation.9 | async-start | bytes 1474560 | tf_op jit(solution)/shard_map/all_gather | solution.py:255
  2077.3 777.2 %all-reduce.20.cloned.1.call-start = ((), (), s32[]{:S(2)}) async-start(), calls=%async_computation.18 | async-start | bytes 25165824 | tf_op jit(solution)/shard_map/psum | solution.py:169
  2102.7 845.9 %all-gather.11.cloned.1.call-start = ((), (), s32[]{:S(2)}) async-start(), calls=%async_computation.14 | async-start | bytes 18874368 | tf_op jit(solution)/shard_map/all_gather | solution.py:260
  2274.6 269.0 %copy-start.57 = (u32[32]{0:T(128)S(1)}, u32[32]{0:T(128)}, u32[]{:S(2)}) copy-start(u32[32]{0:T(128)} %constant.261) | copy-start | bytes 388
  2279.4 51.1 %collective-permute-start = (f32[2,256,2,1024]{3,2,1,0:T(2,128)S(1)}, f32[2,256,2,1024]{3,2,1,0:T(2,128)S(1)}, u32[]{:S(2)}, u32[]{:S(2)}) collective-permute-start(f32[2,256,2,1024]{3,2,1,0:T(2,128)S(1)} %get-tuple-element.673), channel_id=1, source_target_pairs={{0,4},{4,8},{8,12},{12,16},{16,20},{20,24},{24,28},{28,0},{1,5},{5... | collective-permute-start | bytes 12582920 | tf_op jit(solution)/shard_map/ppermute | solution.py:18
  2332.4 50.5 %collective-permute-start.1 = (f32[2,256,2,1024]{3,2,1,0:T(2,128)S(1)}, f32[2,256,2,1024]{3,2,1,0:T(2,128)S(1)}, u32[]{:S(2)}, u32[]{:S(2)}) collective-permute-start(f32[2,256,2,1024]{3,2,1,0:T(2,128)S(1)} %collective-permute-done), channel_id=1, source_target_pairs={{0,4},{4,8},{8,12},{12,16},{16,20},{20,24},{24,28},{28,0},{1,5},{5... | collective-permute-start | bytes 12582920 | tf_op jit(solution)/shard_map/ppermute | solution.py:18
  2385.0 56.9 %collective-permute-start.2 = (f32[2,256,2,1024]{3,2,1,0:T(2,128)S(1)}, f32[2,256,2,1024]{3,2,1,0:T(2,128)S(1)}, u32[]{:S(2)}, u32[]{:S(2)}) collective-permute-start(f32[2,256,2,1024]{3,2,1,0:T(2,128)S(1)} %collective-permute-done.1), channel_id=1, source_target_pairs={{0,4},{4,8},{8,12},{12,16},{16,20},{20,24},{24,28},{28,0},{1,5},{5... | collective-permute-start | bytes 12582920 | tf_op jit(solution)/shard_map/ppermute | solution.py:18
  2443.8 48.8 %collective-permute-start.3 = (f32[2,256,2,1024]{3,2,1,0:T(2,128)S(1)}, f32[2,256,2,1024]{3,2,1,0:T(2,128)S(1)}, u32[]{:S(2)}, u32[]{:S(2)}) collective-permute-start(f32[2,256,2,1024]{3,2,1,0:T(2,128)S(1)} %collective-permute-done.2), channel_id=1, source_target_pairs={{0,4},{4,8},{8,12},{12,16},{16,20},{20,24},{24,28},{28,0},{1,5},{5... | collective-permute-start | bytes 12582920 | tf_op jit(solution)/shard_map/ppermute | solution.py:18
  2494.6 48.9 %collective-permute-start.4 = (f32[2,256,2,1024]{3,2,1,0:T(2,128)S(1)}, f32[2,256,2,1024]{3,2,1,0:T(2,128)}, u32[]{:S(2)}, u32[]{:S(2)}) collective-permute-start(f32[2,256,2,1024]{3,2,1,0:T(2,128)S(1)} %collective-permute-done.3), channel_id=1, source_target_pairs={{0,4},{4,8},{8,12},{12,16},{16,20},{20,24},{24,28},{28,0},{1,5},{5... | collective-permute-start | bytes 12582920 | tf_op jit(solution)/shard_map/ppermute | solution.py:18
  2543.6 51.0 %collective-permute-start.5 = (f32[2,256,2,1024]{3,2,1,0:T(2,128)}, f32[2,256,2,1024]{3,2,1,0:T(2,128)}, u32[]{:S(2)}, u32[]{:S(2)}) collective-permute-start(f32[2,256,2,1024]{3,2,1,0:T(2,128)} %collective-permute-done.4), channel_id=1, source_target_pairs={{0,4},{4,8},{8,12},{12,16},{16,20},{20,24},{24,28},{28,0},{1,5},{5... | collective-permute-start | bytes 12582920 | tf_op jit(solution)/shard_map/ppermute | solution.py:18
  2594.5 381.8 %collective-permute-start.6 = (f32[2,256,2,1024]{3,2,1,0:T(2,128)}, f32[2,256,2,1024]{3,2,1,0:T(2,128)}, u32[]{:S(2)}, u32[]{:S(2)}) collective-permute-start(f32[2,256,2,1024]{3,2,1,0:T(2,128)} %collective-permute-done.5), channel_id=1, source_target_pairs={{0,4},{4,8},{8,12},{12,16},{16,20},{20,24},{24,28},{28,0},{1,5},{5... | collective-permute-start | bytes 12582920 | tf_op jit(solution)/shard_map/ppermute | solution.py:18
  (62 other events, 644.8 us)
Sparse Core Ops, SparseCore 0:
  89.3 40.5 all-reduce.17
  1828.9 35.8 reduce-scatter.16
  1868.9 37.2 reduce-scatter.14
  1910.1 115.9 reduce-scatter.20
  2051.3 204.7 reduce-scatter.22
  2259.0 34.8 reduce-scatter.26
  2297.9 34.3 reduce-scatter.24
  2335.9 31.6 reduce-scatter.18
  2369.7 26.0 all-gather.8
  2397.7 27.4 all-gather.6
  2428.5 425.8 all-reduce.19
  2856.3 92.2 all-gather.10
